TPU v7x, 32 devices: a whole 2x2x4 slice. The times are simulated.
32 devices in a mesh: dp: 16 (over z, y, x), mp: 2 (over core).
Axes of the slice: x: 2, y: 2, z: 4, core: 2. Of those that a mesh axis runs over, the one named last changes fastest.
Arguments:
- inputs_blk: bfloat16 [4096, 4, 512], P('dp', 'mp'), may hold values from -6 to 6
- grads_out: bfloat16 [4096, 4, 512], P('dp', 'mp'), may hold values from -0.09375 to 0.09375
- assign: int32 [4], replicated, may hold values from 0 to 1, as said below
- param_owner: int32 [4], replicated, may hold values from 0 to 1, as said below
- left_root: bfloat16 [6, 512, 512], P('mp', 'dp'), as said below
- right_root: bfloat16 [6, 512, 512], P('mp'), as said below
- momentum: float32 [6, 512, 512], P('mp', 'dp'), may hold values from -6 to 6
Outputs:
- new_momentum: float32 [6, 512, 512], P('mp', 'dp')
- update: bfloat16 [6, 512, 512], P('mp', 'dp')
Inputs may be any that keep to these rules, and one draw needn't show every extreme that they name: `assign`: no index owns more than 3 blocks, and one owns exactly 3. `param_owner`: no index owns more than 3 blocks, and one owns exactly 3. `left_root`: each matrix is symmetric positive definite. `right_root`: each matrix is symmetric positive definite.
All inputs are finite; a program needn't handle non-finite values.
Results may differ from a plain program's by a relative error of at most 0.0013.
The roundings to bfloat16 on the way count: a program that leaves them out, or rounds other values in their place, can miss the bound.
Values may be sent and summed in bfloat16 or wider, within the bound.
A program may use at most 64 MiB of HBM per device.

v0:
```python
import jax
import jax.numpy as jnp
from jax import lax
from jax.sharding import PartitionSpec as P

BETA = 0.9
EPS = 1e-06


def slots_of(owners):
    block_ids = jnp.arange(owners.shape[0], dtype=jnp.int32)
    same = (owners[None, :] == owners[:, None]) & (block_ids[None, :] < block_ids[:, None])
    return jnp.sum(same.astype(jnp.int32), axis=1)


def on_device(inputs_blk, grads_out, assign, param_owner, left_root, right_root, momentum):
    capacity = right_root.shape[0]
    blocks = assign.shape[0]
    my_index = lax.axis_index("mp")
    window = inputs_blk
    reduced = lax.psum_scatter(
        jnp.einsum("tkr,tkc->rkc", window, grads_out, preferred_element_type=jnp.float32),
        "dp",
        scatter_dimension=0,
        tiled=True,
    )
    rounded = reduced.astype(jnp.bfloat16)
    gathered = lax.all_gather(rounded, "mp", axis=1, tiled=True)
    slot = slots_of(assign)
    slot_ids = lax.broadcasted_iota(jnp.int32, (capacity, blocks), 0)
    chooser = ((assign[None, :] == my_index) & (slot[None, :] == slot_ids)).astype(jnp.bfloat16)
    owned = jnp.einsum("ck,rkb->crb", chooser, gathered, preferred_element_type=jnp.float32).astype(
        jnp.bfloat16
    )
    half = jnp.einsum("crb,cbe->cre", owned, right_root, preferred_element_type=jnp.float32).astype(
        jnp.bfloat16
    )
    window = left_root
    both = jnp.einsum(
        "cri,cie->cre",
        window,
        lax.all_gather(half, "dp", axis=1, tiled=True),
        preferred_element_type=jnp.float32,
    )
    grad_square = jnp.sum(jnp.square(owned.astype(jnp.float32)), axis=(1, 2))
    prec_square = jnp.sum(both * both, axis=(1, 2))
    grad_square, prec_square = lax.psum((grad_square, prec_square), "dp")
    factor = jnp.sqrt(grad_square / (prec_square + EPS))
    moved = BETA * momentum + both * factor[:, None, None]
    sending = moved.astype(jnp.bfloat16)
    pooled = lax.all_gather(sending, "mp", axis=0, tiled=True)
    place = slots_of(param_owner)
    source = assign * capacity + slot
    target_hot = ((param_owner[None, :] == my_index) & (place[None, :] == slot_ids)).astype(
        jnp.float32
    )
    pool_ids = lax.broadcasted_iota(jnp.int32, (blocks, pooled.shape[0]), 1)
    source_hot = (source[:, None] == pool_ids).astype(jnp.float32)
    mover = jnp.dot(target_hot, source_hot, preferred_element_type=jnp.float32).astype(jnp.bfloat16)
    update = jnp.einsum("qs,srb->qrb", mover, pooled, preferred_element_type=jnp.float32).astype(
        jnp.bfloat16
    )
    return (moved, update)


def solution(mesh):
    placed = (
        P("dp", "mp", None),
        P("dp", "mp", None),
        P(),
        P(),
        P("mp", "dp", None),
        P("mp", None, None),
        P("mp", "dp", None),
    )
    return jax.shard_map(
        on_device,
        mesh=mesh,
        in_specs=placed,
        out_specs=(P("mp", "dp", None), P("mp", "dp", None)),
        check_vma=False,
    )
```

profile of v0, /device:TPU:1, one launch (start us, length us, event | category | flops | bytes accessed | tf_op | source)
XLA Modules:
  0.0 229.7 jit_solution(6821913359168014686)
XLA Ops:
  7.2 0.0 copy-start
  7.2 0.0 all-gather.2.cloned.1.call-start
  7.2 3.1 %convolution_bitcast_fusion = f32[512,2,512]{0,2,1:T(8,128)} fusion(bf16[256,2,512]{2,1,0:T(2,128)(2,1)} %param.7, bf16[256,2,512]{2,1,0:T(2,128)(2,1)} %param.8), kind=kOutput, calls=%fused_computation | convolution fusion | flops 268435456 | bytes 3145728 | tf_op jit(solution)/shard_map/tkr,tkc->rkc/dot_general | solution.py:22
  10.4 4.1 %copy.17 = f32[512,2,512]{2,1,0:T(2,128)} copy(f32[512,2,512]{0,2,1:T(8,128)} %convolution_bitcast_fusion) | data formatting | bytes 4194304 | tf_op jit(solution)/shard_map/tkr,tkc->rkc/transpose | solution.py:22
  14.5 0.0 copy-start.5
  14.5 0.0 copy-start.4
  14.5 94.0 %all-reduce.3 = bf16[512,2,512]{2,1,0:T(2,128)(2,1)S(1)} all-reduce(f32[512,2,512]{2,1,0:T(2,128)} %copy.17), channel_id=2, replica_groups=mesh['dp'=16,'mp'=2] {'dp'}, use_global_device_ids=true, to_apply=%region_1.0.clone | all-reduce | flops 524288 | bytes 3145728
  108.5 0.0 copy-start.3
  108.5 0.0 copy-start.2
  108.6 0.0 copy-done.5
  108.6 0.6 dynamic-slice
  109.8 0.1 dynamic-slice_convert_fusion
  109.9 9.0 %all_gather.9 = bf16[32,4,512]{2,0,1:T(8,128)(2,1)S(1)} all-gather(bf16[32,2,512]{2,0,1:T(8,128)(2,1)S(1)} %copy.18), channel_id=1, replica_groups=mesh['dp'=16,'mp'=2] {'mp'}, dimensions={1}, use_global_device_ids=true | all-gather | bytes 196608 | tf_op jit(solution)/shard_map/all_gather | solution.py:28
  118.9 0.0 copy-done.4
  118.9 0.2 convert_reduce_fusion.1
  119.1 0.4 multiply_reduce_fusion
  119.5 0.0 copy-done
  119.5 0.0 copy-start.1
  119.5 1.0 convolution_convert_fusion.2
  120.5 0.0 all-gather.2.cloned.1.call-update
  120.6 0.0 copy-done.3
  120.6 0.2 convert_reduce_fusion
  120.8 55.1 %all-gather.2.cloned.1.call-done = bf16[3,512,512]{2,1,0:T(8,128)(2,1)} async-done(((bf16[3,32,512]{2,1,0:T(8,128)(2,1)}), bf16[3,512,512]{2,1,0:T(8,128)(2,1)}) %all-gather.2.cloned.1.call-update) | async-done | bytes 1572880 | tf_op jit(solution)/shard_map/all_gather | solution.py:42
  175.8 0.0 copy-done.2
  175.8 1.9 multiply_reduce_fusion.1
  177.7 31.8 %all-reduce.1 = (f32[3]{0:T(128)S(1)}, f32[3]{0:T(128)S(1)}) all-reduce(f32[3]{0:T(128)S(1)} %get-tuple-element.12, f32[3]{0:T(128)S(1)} %get-tuple-element.14), channel_id=1, replica_groups=mesh['dp'=16,'mp'=2] {'dp'}, use_global_device_ids=true, to_apply=%region_3.0 | all-reduce | flops 6 | bytes 48 | tf_op jit(solution)/shard_map/psum | solution.py:47
  209.5 0.0 copy-done.1
  209.5 0.8 fusion.23
  210.3 11.5 %all_gather.11 = bf16[6,32,512]{2,1,0:T(8,128)(2,1)S(1)} all-gather(bf16[3,32,512]{2,1,0:T(8,128)(2,1)S(1)} %get-tuple-element.10), channel_id=1, replica_groups=mesh['dp'=16,'mp'=2] {'mp'}, dimensions={0}, use_global_device_ids=true | all-gather | bytes 294912 | tf_op jit(solution)/shard_map/all_gather | solution.py:51
  221.8 0.4 convolution_convert_fusion.1
  222.2 0.7 copy.22
  (5 shorter events, 0.0 us)
Async XLA Ops:
  7.2 112.3 %copy-start = (bf16[3,512,512]{2,1,0:T(8,128)(2,1)S(1)}, bf16[3,512,512]{2,1,0:T(8,128)(2,1)}, u32[]{:S(2)}) copy-start(bf16[3,512,512]{2,1,0:T(8,128)(2,1)} %param.12) | copy-start | bytes 4718596
  7.2 168.6 %all-gather.2.cloned.1.call-start = ((), (), s32[]{:S(2)}) async-start(), calls=%async_computation | async-start | bytes 1671168 | tf_op jit(solution)/shard_map/all_gather | solution.py:42
  14.5 94.1 %copy-start.5 = (u32[32]{0:T(128)S(1)}, u32[32]{0:T(128)}, u32[]{:S(2)}) copy-start(u32[32]{0:T(128)} %constant.19) | copy-start | bytes 388
  14.5 104.4 %copy-start.4 = (s32[4]{0:T(128)S(1)}, s32[4]{0:T(128)}, u32[]{:S(2)}) copy-start(s32[4]{0:T(128)} %param.9) | copy-start | bytes 52
  108.5 12.0 %copy-start.3 = (s32[4]{0:T(128)S(1)}, s32[4]{0:T(128)}, u32[]{:S(2)}) copy-start(s32[4]{0:T(128)} %param.10) | copy-start | bytes 52
  108.5 67.3 %copy-start.2 = (bf16[3,32,512]{2,1,0:T(8,128)(2,1)S(1)}, bf16[3,32,512]{2,1,0:T(8,128)(2,1)}, u32[]{:S(2)}) copy-start(bf16[3,32,512]{2,1,0:T(8,128)(2,1)} %param.11) | copy-start | bytes 294916
  119.5 90.0 %copy-start.1 = (f32[3,32,512]{2,1,0:T(8,128)S(1)}, f32[3,32,512]{2,1,0:T(8,128)}, u32[]{:S(2)}) copy-start(f32[3,32,512]{2,1,0:T(8,128)} %param.13) | copy-start | bytes 589828
Sparse Core Ops, SparseCore 0:
  120.7 55.1 all-gather.1
where the time goes:
time: 230 us
  blocking collectives  146 us (63%)
  waiting for transfers between devices  55.1 us (24%)
  between operations  14.8 us (6%)
  matrix products  6.81 us (3%)
  local copies, waits for them, and re-layouts  5.48 us (2%)
    unnamed x1, blocking collectives  94 us
    all_gather x1, waiting for transfers between devices, on_device(): lax.all_gather(half, 'dp', axis=1, tiled=True)  55.1 us
    psum x1, blocking collectives, on_device(): grad_square, prec_square = lax.psum((grad_square, prec_square), 'dp')  31.8 us
    all_gather x1, blocking collectives, on_device(): pooled = lax.all_gather(sending, 'mp', axis=0, tiled=True)  11.5 us
    all_gather x1, blocking collectives, on_device(): gathered = lax.all_gather(rounded, 'mp', axis=1, tiled=True)  9.02 us
  transfers between devices with their start and end apart: 1, of which 1 were waited for; matrix products, arithmetic and copies ran while one was open for 0% of the time, Pallas kernels for 0%

commit v1 on v0

v1 whole, which is shorter than its diff:
```python
import functools

import jax
import jax.numpy as jnp
from jax import lax
from jax.experimental import pallas as pl
from jax.experimental.pallas import tpu as pltpu
from jax.sharding import PartitionSpec as P

BETA = 0.9
EPS = 1e-06
QUAD = 4
PARTS = 2
MESH = pl.DeviceIdType.MESH
F32 = jnp.float32
BF16 = jnp.bfloat16


def slots_of(owners):
    block_ids = jnp.arange(owners.shape[0], dtype=jnp.int32)
    same = (owners[None, :] == owners[:, None]) & (block_ids[None, :] < block_ids[:, None])
    return jnp.sum(same.astype(jnp.int32), axis=1)


def scalar_places(ref, blocks, capacity):
    owners = [ref[k] for k in range(blocks)]
    places = []
    for k in range(blocks):
        count = owners[k] * capacity
        for j in range(k):
            count = count + jnp.where(owners[j] == owners[k], 1, 0)
        places.append(count)
    return places


def hot(a, b):
    return jnp.where(a == b, 1.0, 0.0).astype(F32)


def kernel(
    dims,
    x_ref, y_ref, assign_ref, owner_ref, left_hbm, right_hbm, mom_hbm,
    mom_out, upd_out,
    g_ref, r1_ref, t_ref, r2_ref, full_ref, right_ref, left_ref, mom_ref,
    rsel_ref, lsel_ref, msel_ref, both_ref, p_ref, pr_ref,
    local_sem, pre_send, pre_recv, s1_send, s1_recv, s2_send, s2_recv, s3_send, s3_recv,
    s4_send, s4_recv, fw_send, fw_recv, p_send, p_recv,
):
    n_dp, mine, blocks, capacity, size = dims
    lines = n_dp // QUAD
    rows = size // n_dp
    band = size // QUAD
    width = size // PARTS
    chunks = mine * PARTS
    me = lax.axis_index("dp")
    core = lax.axis_index("mp")
    q = lax.rem(me, QUAD)
    z = me // QUAD
    other = 1 - core

    def at_quad(j):
        return (z * QUAD + lax.rem(q + j, QUAD), core)

    def at_line(j):
        return (lax.rem(z + j, lines) * QUAD + q, core)

    barrier = pltpu.get_barrier_semaphore()
    for j in range(1, n_dp):
        pl.semaphore_signal(barrier, inc=1, device_id=(lax.rem(me + j, n_dp), core), device_id_type=MESH)
    pl.semaphore_signal(barrier, inc=1, device_id=(me, other), device_id_type=MESH)

    own = pl.ds(core * capacity, capacity)
    theirs = pl.ds(other * capacity, capacity)
    stored = ((right_hbm, right_ref), (left_hbm, left_ref), (mom_hbm, mom_ref))
    local = [
        pltpu.make_async_copy(src, dst.at[own], local_sem.at[i]) for i, (src, dst) in enumerate(stored)
    ]
    for copy in local:
        copy.start()

    def multiply(c):
        k, h = divmod(c, PARTS)
        x = x_ref[:, k * size:(k + 1) * size]
        y = y_ref[:, k * size + h * width:k * size + (h + 1) * width]
        g_ref[c] = lax.dot_general(x, y, (((0,), (0,)), ((), ())), preferred_element_type=F32)

    sends = []

    def remote(src, dst, send, recv, device):
        return pltpu.make_async_remote_copy(
            src_ref=src, dst_ref=dst, send_sem=send, recv_sem=recv, device_id=device, device_id_type=MESH
        )

    def start(copy):
        copy.start()
        sends.append(copy)

    def s1(c):
        for j in range(1, QUAD):
            band_at = pl.ds(lax.rem(q + j, QUAD) * band, band)
            start(remote(g_ref.at[c, band_at], r1_ref.at[c, j - 1], s1_send.at[c, j - 1], s1_recv.at[c, j - 1], at_quad(j)))

    def s2(c):
        for j in range(1, QUAD):
            remote(r1_ref.at[c, j - 1], r1_ref.at[c, j - 1], s1_send.at[c, j - 1], s1_recv.at[c, j - 1], at_quad(j)).wait_recv()
        total = g_ref[c, pl.ds(q * band, band), :]
        for j in range(1, QUAD):
            total = total + r1_ref[c, j - 1]
        t_ref[c] = total
        for j in range(1, lines):
            rows_at = pl.ds(lax.rem(z + j, lines) * rows, rows)
            start(remote(t_ref.at[c, rows_at], r2_ref.at[c, j - 1], s2_send.at[c, j - 1], s2_recv.at[c, j - 1], at_line(j)))

    def s3(c):
        for j in range(1, lines):
            remote(r2_ref.at[c, j - 1], r2_ref.at[c, j - 1], s2_send.at[c, j - 1], s2_recv.at[c, j - 1], at_line(j)).wait_recv()
        total = t_ref[c, pl.ds(z * rows, rows), :]
        for j in range(1, lines):
            total = total + r2_ref[c, j - 1]
        g = core * chunks + c
        mine_at = pl.ds(q * band + z * rows, rows)
        full_ref[g, mine_at, :] = total.astype(BF16)
        piece = full_ref.at[g, mine_at]
        for j in range(1, lines):
            start(remote(piece, piece, s3_send.at[c, j - 1], s3_recv.at[c, j - 1], at_line(j)))

    def s4(c):
        g = core * chunks + c
        for j in range(1, lines):
            source = lax.rem(z + lines - j, lines)
            piece = full_ref.at[g, pl.ds(q * band + source * rows, rows)]
            remote(piece, piece, s3_send.at[c, j - 1], s3_recv.at[c, j - 1], at_line(j)).wait_recv()
        piece = full_ref.at[g, pl.ds(q * band, band)]
        for j in range(1, QUAD):
            start(remote(piece, piece, s4_send.at[c, j - 1], s4_recv.at[c, j - 1], at_quad(j)))
        start(remote(piece, piece, fw_send.at[c, 0], fw_recv.at[c, 0], (me, other)))

    def s5(c):
        g = core * chunks + c
        for j in range(1, QUAD):
            source = lax.rem(q + QUAD - j, QUAD)
            piece = full_ref.at[g, pl.ds(source * band, band)]
            remote(piece, piece, s4_send.at[c, j - 1], s4_recv.at[c, j - 1], at_quad(j)).wait_recv()
            start(remote(piece, piece, fw_send.at[c, j], fw_recv.at[c, j], (me, other)))

    def s6(c):
        g = other * chunks + c
        for j in range(QUAD):
            source = lax.rem(q + QUAD - j, QUAD)
            piece = full_ref.at[g, pl.ds(source * band, band)]
            remote(piece, piece, fw_send.at[c, j], fw_recv.at[c, j], (me, other)).wait_recv()

    multiply(0)
    pl.semaphore_wait(barrier, n_dp)
    s1(0)
    for c in range(1, chunks):
        multiply(c)
        s1(c)
    for i, (src, dst) in enumerate(stored):
        start(remote(src, dst.at[own], pre_send.at[i], pre_recv.at[i], (me, other)))

    index = scalar_places(assign_ref, blocks, capacity)
    target = scalar_places(owner_ref, blocks, capacity)
    for copy in local:
        copy.wait()
    for i, (src, dst) in enumerate(stored):
        remote(src, dst.at[theirs], pre_send.at[i], pre_recv.at[i], (me, other)).wait_recv()

    slots = 2 * capacity
    for k in range(blocks):
        picks = [hot(index[k], s) for s in range(slots)]

        def pick(at, _, k=k, picks=picks):
            part = pl.ds(pl.multiple_of(at * 64, 64), 64)
            chosen = right_ref[0, part, :].astype(F32) * picks[0]
            for s in range(1, slots):
                chosen = chosen + right_ref[s, part, :].astype(F32) * picks[s]
            rsel_ref[k, part, :] = chosen.astype(BF16)
            return 0

        lax.fori_loop(0, size // 64, pick, 0)
        chosen = left_ref[0].astype(F32) * picks[0]
        moment = mom_ref[0] * picks[0]
        for s in range(1, slots):
            chosen = chosen + left_ref[s].astype(F32) * picks[s]
            moment = moment + mom_ref[s] * picks[s]
        lsel_ref[k] = chosen.astype(BF16)
        msel_ref[k] = moment

    stages = (s2, s3, s4, s5)
    for step in range(chunks + len(stages) - 1):
        for late in reversed(range(len(stages))):
            c = step - late
            if 0 <= c < chunks:
                stages[late](c)
    for c in range(chunks):
        s6(c)

    def precondition(k, _):
        half = jnp.zeros((size, size), F32)
        for h in range(PARTS):
            half = half + jnp.dot(
                full_ref[k * PARTS + h], rsel_ref[k, h * width:(h + 1) * width, :], preferred_element_type=F32
            )
        both_ref[k] = jnp.dot(lsel_ref[k], half.astype(BF16), preferred_element_type=F32)
        return 0

    lax.fori_loop(0, blocks, precondition, 0)

    def lanes(value):
        partial = value[:, 0:128]
        for at in range(128, value.shape[1], 128):
            partial = partial + value[:, at:at + 128]
        return jnp.sum(partial, axis=0, keepdims=True)

    p_ref[...] = jnp.zeros_like(p_ref)
    for k in range(blocks):
        both = both_ref[k]
        p_ref[k:k + 1, :] = lanes(both * both)
    for j in range(1, n_dp):
        start(remote(p_ref, pr_ref.at[j - 1], p_send.at[j - 1], p_recv.at[j - 1], (lax.rem(me + j, n_dp), core)))

    grad_square = []
    for k in range(blocks):
        def add(at, total, k=k):
            part = pl.ds(pl.multiple_of(at * 64, 64), 64)
            for h in range(PARTS):
                value = full_ref[k * PARTS + h, part, :].astype(F32)
                total = total + lanes(value * value)
            return total

        lane_sum = lax.fori_loop(0, size // 64, add, jnp.zeros((1, 128), F32))
        grad_square.append(jnp.sum(lane_sum, axis=1, keepdims=True))

    for j in range(1, n_dp):
        remote(p_ref, pr_ref.at[j - 1], p_send.at[j - 1], p_recv.at[j - 1], (lax.rem(me + j, n_dp), core)).wait_recv()
    total = p_ref[...]
    for j in range(1, n_dp):
        total = total + pr_ref[j - 1]
    prec_square = jnp.sum(total, axis=1, keepdims=True)
    grafted = [
        both_ref[k] * jnp.sqrt(grad_square[k] / (prec_square[k:k + 1, :] + EPS)) for k in range(blocks)
    ]
    moved = [(BETA * msel_ref[k] + grafted[k]).astype(BF16).astype(F32) for k in range(blocks)]
    for s in range(capacity):
        here = core * capacity + s
        value = BETA * mom_ref[here]
        update = jnp.zeros((rows, size), F32)
        for k in range(blocks):
            value = value + grafted[k] * hot(index[k], here)
            update = update + moved[k] * hot(target[k], here)
        mom_out[s] = value
        upd_out[s] = update.astype(BF16)
    for copy in sends:
        copy.wait_send()


def fused(n_dp, inputs_blk, grads_out, assign, param_owner, left_root, right_root, momentum):
    tokens, mine, size = inputs_blk.shape
    capacity = right_root.shape[0]
    blocks = assign.shape[0]
    rows = size // n_dp
    band, width, lines = size // QUAD, size // PARTS, n_dp // QUAD
    chunks = mine * PARTS
    slots = 2 * capacity
    vmem = pl.BlockSpec(memory_space=pltpu.VMEM)
    smem = pl.BlockSpec(memory_space=pltpu.SMEM)
    anyw = pl.BlockSpec(memory_space=pl.ANY)
    dma = pltpu.SemaphoreType.DMA
    flops = 2 * mine * tokens * size * size + 2 * blocks * size**3
    return pl.pallas_call(
        functools.partial(kernel, (n_dp, mine, blocks, capacity, size)),
        out_shape=(
            jax.ShapeDtypeStruct((capacity, rows, size), F32),
            jax.ShapeDtypeStruct((capacity, rows, size), BF16),
        ),
        in_specs=[vmem, vmem, smem, smem, anyw, anyw, anyw],
        out_specs=(vmem, vmem),
        scratch_shapes=[
            pltpu.VMEM((chunks, size, width), F32),
            pltpu.VMEM((chunks, QUAD - 1, band, width), F32),
            pltpu.VMEM((chunks, band, width), F32),
            pltpu.VMEM((chunks, lines - 1, rows, width), F32),
            pltpu.VMEM((2 * chunks, size, width), BF16),
            pltpu.VMEM((slots, size, size), BF16),
            pltpu.VMEM((slots, rows, size), BF16),
            pltpu.VMEM((slots, rows, size), F32),
            pltpu.VMEM((blocks, size, size), BF16),
            pltpu.VMEM((blocks, rows, size), BF16),
            pltpu.VMEM((blocks, rows, size), F32),
            pltpu.VMEM((blocks, rows, size), F32),
            pltpu.VMEM((8, 128), F32),
            pltpu.VMEM((n_dp - 1, 8, 128), F32),
            dma((3,)), dma((3,)), dma((3,)),
            dma((chunks, QUAD - 1)), dma((chunks, QUAD - 1)),
            dma((chunks, lines - 1)), dma((chunks, lines - 1)),
            dma((chunks, lines - 1)), dma((chunks, lines - 1)),
            dma((chunks, QUAD - 1)), dma((chunks, QUAD - 1)),
            dma((chunks, QUAD)), dma((chunks, QUAD)),
            dma((n_dp - 1,)), dma((n_dp - 1,)),
        ],
        compiler_params=pltpu.CompilerParams(
            collective_id=0, has_side_effects=True, vmem_limit_bytes=40 * 1024 * 1024
        ),
        cost_estimate=pl.CostEstimate(flops=flops, bytes_accessed=4 * 1024 * 1024, transcendentals=0),
    )(
        inputs_blk.reshape(tokens, mine * size),
        grads_out.reshape(tokens, mine * size),
        assign, param_owner, left_root, right_root, momentum,
    )


def general(inputs_blk, grads_out, assign, param_owner, left_root, right_root, momentum):
    capacity = right_root.shape[0]
    blocks = assign.shape[0]
    my_index = lax.axis_index("mp")
    reduced = lax.psum_scatter(
        jnp.einsum("tkr,tkc->rkc", inputs_blk, grads_out, preferred_element_type=F32),
        "dp",
        scatter_dimension=0,
        tiled=True,
    )
    rounded = reduced.astype(BF16)
    gathered = lax.all_gather(rounded, "mp", axis=1, tiled=True)
    slot = slots_of(assign)
    slot_ids = lax.broadcasted_iota(jnp.int32, (capacity, blocks), 0)
    chooser = ((assign[None, :] == my_index) & (slot[None, :] == slot_ids)).astype(BF16)
    owned = jnp.einsum("ck,rkb->crb", chooser, gathered, preferred_element_type=F32).astype(BF16)
    half = jnp.einsum("crb,cbe->cre", owned, right_root, preferred_element_type=F32).astype(BF16)
    both = jnp.einsum(
        "cri,cie->cre",
        left_root,
        lax.all_gather(half, "dp", axis=1, tiled=True),
        preferred_element_type=F32,
    )
    grad_square = jnp.sum(jnp.square(owned.astype(F32)), axis=(1, 2))
    prec_square = jnp.sum(both * both, axis=(1, 2))
    grad_square, prec_square = lax.psum((grad_square, prec_square), "dp")
    factor = jnp.sqrt(grad_square / (prec_square + EPS))
    moved = BETA * momentum + both * factor[:, None, None]
    sending = moved.astype(BF16)
    pooled = lax.all_gather(sending, "mp", axis=0, tiled=True)
    place = slots_of(param_owner)
    source = assign * capacity + slot
    target_hot = ((param_owner[None, :] == my_index) & (place[None, :] == slot_ids)).astype(F32)
    pool_ids = lax.broadcasted_iota(jnp.int32, (blocks, pooled.shape[0]), 1)
    source_hot = (source[:, None] == pool_ids).astype(F32)
    mover = jnp.dot(target_hot, source_hot, preferred_element_type=F32).astype(BF16)
    update = jnp.einsum("qs,srb->qrb", mover, pooled, preferred_element_type=F32).astype(BF16)
    return (moved, update)


def solution(mesh):
    n_dp, n_mp = mesh.shape["dp"], mesh.shape["mp"]

    def on_device(inputs_blk, *rest):
        rows = inputs_blk.shape[2] // n_dp
        if n_mp == 2 and n_dp % QUAD == 0 and rows % 16 == 0:
            return fused(n_dp, inputs_blk, *rest)
        return general(inputs_blk, *rest)

    placed = (
        P("dp", "mp", None),
        P("dp", "mp", None),
        P(),
        P(),
        P("mp", "dp", None),
        P("mp", None, None),
        P("mp", "dp", None),
    )
    return jax.shard_map(
        on_device,
        mesh=mesh,
        in_specs=placed,
        out_specs=(P("mp", "dp", None), P("mp", "dp", None)),
        check_vma=False,
    )
```

time: 230 us -> 60.6 us (0.26)
  blocking collectives: 146 us -> 0 us
  Pallas kernels: 0 us -> 55.9 us
  waiting for transfers between devices: 55.1 us -> 0 us
  between operations: 14.8 us -> 0.73 us
  matrix products: 6.81 us -> 0 us
    unnamed x1 -> x0, blocking collectives: 94 us -> none
    pallas_call x0 -> x1, Pallas kernels: none -> 55.9 us  [fused(): pl.pallas_call(functools.partial(kernel, (n_dp, mine, blocks, capacity, s...]
    all_gather x1 -> x0, waiting for transfers between devices: 55.1 us -> none  [on_device(): lax.all_gather(half, 'dp', axis=1, tiled=True)]
    psum x1 -> x0, blocking collectives: 31.8 us -> none  [on_device(): grad_square, prec_square = lax.psum((grad_square, prec_square), 'dp')]
    all_gather x2 -> x0, blocking collectives: 20.5 us -> none  [the longest x1 11.5 us: on_device(): pooled = lax.all_gather(sending, 'mp', axis=0, tiled=True)]
    dot_general x5 -> x0, matrix products: 6.81 us -> none  [the longest x1 3.15 us: on_device(): jnp.einsum('tkr,tkc->rkc', window, grads_out, preferred_element_type=jnp....]
    transpose x1 -> x0, local copies, waits for them, and re-layouts: 4.13 us -> none  [on_device(): jnp.einsum('tkr,tkc->rkc', window, grads_out, preferred_element_type=jnp....]
    unnamed x14, local copies, waits for them, and re-layouts: 1.28 us -> 3.69 us
  transfers between devices with their start and end apart: 1 -> 0, of which waited for: 1 -> 0; matrix products, arithmetic and copies ran while one was open for 0% -> 0% of each run, Pallas kernels for 0% -> 0%
where the time goes in v1:
time: 60.6 us; the launch traced here: 60.3 us
  Pallas kernels  55.9 us (92%)
  local copies, waits for them, and re-layouts  3.69 us (6%)
  between operations  0.73 us (1%)
    pallas_call x1, Pallas kernels, fused(): pl.pallas_call(functools.partial(kernel, (n_dp, mine, blocks, capacity, s...  55.9 us
    unnamed x14, local copies, waits for them, and re-layouts  3.69 us

profile of v1, /device:TPU:1, one launch (start us, length us, event | category | flops | bytes accessed | tf_op | source)
XLA Modules:
  0.0 60.3 jit_solution(8366926508934975960)
XLA Ops:
  0.6 0.0 copy-start.1
  0.6 0.0 copy-start
  0.7 0.0 copy-start.2
  0.7 0.0 copy-start.4
  0.7 0.0 copy-start.3
  0.7 1.2 %copy.9 = bf16[32,8,2,512]{3,1,2,0:T(8,128)(2,1)S(1)} copy(bf16[32,8,2,512]{3,2,1,0:T(2,128)(2,1)} %bitcast.6) | data formatting | bytes 1048576
  1.9 1.1 %copy.10 = bf16[32,8,2,512]{3,1,2,0:T(8,128)(2,1)S(1)} copy(bf16[32,8,2,512]{3,2,1,0:T(2,128)(2,1)} %bitcast.7) | data formatting | bytes 1048576
  3.0 0.0 copy-done.1
  3.1 0.0 copy-done
  3.1 0.0 copy-done.2
  3.1 0.0 copy-done.4
  3.1 0.0 copy-done.3
  3.1 55.9 %shard_map.86 = (f32[3,32,512]{2,1,0:T(8,128)S(1)}, bf16[3,32,512]{2,1,0:T(8,128)(2,1)S(1)}) custom-call(bf16[256,1024]{1,0:T(8,128)(2,1)S(1)} %bitcast.4, bf16[256,1024]{1,0:T(8,128)(2,1)S(1)} %bitcast.5, s32[4]{0:T(128)S(1)} %copy-done.3, s32[4]{0:T(128)S(1)} %copy-done.4, bf16[3,32,512]{2,1,0:T(8,128)(2,1)S(1)} %copy-done.2, ...), custom_call_target="tpu_custom_call" | custom-call | flops 1342177280 | bytes 4194304 | tf_op jit(solution)/shard_map/pallas_call | solution.py:271
  59.0 0.7 %copy.13 = f32[3,32,512]{2,1,0:T(8,128)} copy(f32[3,32,512]{2,1,0:T(8,128)S(1)} %get-tuple-element.4) | data formatting | bytes 393216
  59.7 0.6 %copy.14 = bf16[3,32,512]{2,1,0:T(8,128)(2,1)} copy(bf16[3,32,512]{2,1,0:T(8,128)(2,1)S(1)} %get-tuple-element.5) | data formatting | bytes 196608
Async XLA Ops:
  0.6 2.4 %copy-start.1 = (f32[3,32,512]{2,1,0:T(8,128)S(1)}, f32[3,32,512]{2,1,0:T(8,128)}, u32[]{:S(2)}) copy-start(f32[3,32,512]{2,1,0:T(8,128)} %mom_hbm.1) | copy-start | bytes 589828
  0.6 2.4 %copy-start = (bf16[3,512,512]{2,1,0:T(8,128)(2,1)S(1)}, bf16[3,512,512]{2,1,0:T(8,128)(2,1)}, u32[]{:S(2)}) copy-start(bf16[3,512,512]{2,1,0:T(8,128)(2,1)} %right_hbm.1) | copy-start | bytes 4718596
  0.7 2.4 %copy-start.2 = (bf16[3,32,512]{2,1,0:T(8,128)(2,1)S(1)}, bf16[3,32,512]{2,1,0:T(8,128)(2,1)}, u32[]{:S(2)}) copy-start(bf16[3,32,512]{2,1,0:T(8,128)(2,1)} %left_hbm.1) | copy-start | bytes 294916
  0.7 2.4 %copy-start.4 = (s32[4]{0:T(128)S(1)}, s32[4]{0:T(128)}, u32[]{:S(2)}) copy-start(s32[4]{0:T(128)} %owner_ref.1) | copy-start | bytes 52
  0.7 2.4 %copy-start.3 = (s32[4]{0:T(128)S(1)}, s32[4]{0:T(128)}, u32[]{:S(2)}) copy-start(s32[4]{0:T(128)} %assign_ref.1) | copy-start | bytes 52

commit v2 on v0

v2 whole, which is shorter than its diff:
```python
import functools

import jax
import jax.numpy as jnp
from jax import lax
from jax.experimental import pallas as pl
from jax.experimental.pallas import tpu as pltpu
from jax.sharding import PartitionSpec as P

BETA = 0.9
EPS = 1e-06
PLANE = 4
PARTS = 2
MESH = pl.DeviceIdType.MESH
F32 = jnp.float32
BF16 = jnp.bfloat16


def slots_of(owners):
    block_ids = jnp.arange(owners.shape[0], dtype=jnp.int32)
    same = (owners[None, :] == owners[:, None]) & (block_ids[None, :] < block_ids[:, None])
    return jnp.sum(same.astype(jnp.int32), axis=1)


def scalar_places(ref, blocks, capacity):
    owners = [ref[k] for k in range(blocks)]
    places = []
    for k in range(blocks):
        count = owners[k] * capacity
        for j in range(k):
            count = count + jnp.where(owners[j] == owners[k], 1, 0)
        places.append(count)
    return places


def hot(a, b):
    return jnp.where(a == b, 1.0, 0.0).astype(F32)


def kernel(
    dims,
    x_ref, y_ref, assign_ref, owner_ref, left_hbm, right_hbm, mom_hbm,
    mom_out, upd_out,
    xr_ref, yr_ref, g_ref, r1_ref, t_ref, r2_ref, own_ref, right_ref, left_ref, mom_ref,
    rsel_ref, lband_ref, msel_ref, hb_ref, hall_ref, hfull_ref, bo_ref, both_ref, p_ref, pr_ref, sum_ref,
    local_sem, pre_send, pre_recv, x_send, x_recv, y_send, y_recv, s1_send, s1_recv, s2_send, s2_recv,
    left_send, left_recv, half_send, half_recv, both_send, both_recv, fw_send, fw_recv,
    p_send, p_recv, sum_send, sum_recv,
):
    n_dp, mine, blocks, capacity, size = dims
    lines = n_dp // PLANE
    rows = size // n_dp
    band = size // PLANE
    wing = size // 2
    width = size // PARTS
    me = lax.axis_index("dp")
    core = lax.axis_index("mp")
    q = lax.rem(me, PLANE)
    z = me // PLANE
    x_at, y_at = lax.rem(q, 2), q // 2
    other = 1 - core
    x_mate = (z * PLANE + y_at * 2 + (1 - x_at), core)
    y_mate = (z * PLANE + (1 - y_at) * 2 + x_at, core)
    core_mate = (me, other)

    def plane_mate(j):
        return (z * PLANE + lax.rem(q + j, PLANE), core)

    routes = [
        (x_at, y_at, x_mate, y_mate) if k % 2 == 0 else (y_at, x_at, y_mate, x_mate) for k in range(mine)
    ]

    def at_line(j):
        return (lax.rem(z + j, lines) * PLANE + q, core)

    barrier = pltpu.get_barrier_semaphore()
    partners = [x_mate, y_mate, core_mate] + [at_line(j) for j in range(1, lines)]
    for device in partners:
        pl.semaphore_signal(barrier, inc=1, device_id=device, device_id_type=MESH)

    own = pl.ds(core * capacity, capacity)
    theirs = pl.ds(other * capacity, capacity)
    stored = ((right_hbm, right_ref), (left_hbm, left_ref), (mom_hbm, mom_ref))
    local = [
        pltpu.make_async_copy(src, dst.at[own], local_sem.at[i]) for i, (src, dst) in enumerate(stored)
    ]
    for copy in local:
        copy.start()

    sends = []

    def remote(src, dst, send, recv, device):
        return pltpu.make_async_remote_copy(
            src_ref=src, dst_ref=dst, send_sem=send, recv_sem=recv, device_id=device, device_id_type=MESH
        )

    def start(copy):
        copy.start()
        sends.append(copy)

    def outer(x, y):
        return lax.dot_general(x, y, (((0,), (0,)), ((), ())), preferred_element_type=F32)

    def cols(h):
        return slice(h * width, (h + 1) * width)

    def wing_of(k, a):
        return pl.ds(pl.multiple_of(k * size + a * wing, wing), wing)

    def x_copy(k):
        a, _, mate, _ = routes[k]
        return remote(x_ref.at[:, wing_of(k, 1 - a)], xr_ref.at[k], x_send.at[k], x_recv.at[k], mate)

    def y_copy(k, h):
        src = y_ref.at[:, pl.ds(k * size + h * width, width)]
        return remote(src, yr_ref.at[k, :, pl.ds(h * width, width)], y_send.at[k, h], y_recv.at[k, h], routes[k][2])

    def wing_copy(k, h):
        _, b, _, mate = routes[k]
        src = g_ref.at[k, pl.ds((1 - b) * band, band), pl.ds(h * width, width)]
        return remote(src, r1_ref.at[k, :, pl.ds(h * width, width)], s1_send.at[k, h], s1_recv.at[k, h], mate)

    def line_copy(k, h, j):
        src = t_ref.at[k, pl.ds(lax.rem(z + j, lines) * rows, rows), pl.ds(h * width, width)]
        dst = r2_ref.at[k, j - 1, :, pl.ds(h * width, width)]
        return remote(src, dst, s2_send.at[k, h, j - 1], s2_recv.at[k, h, j - 1], at_line(j))

    def s1(k, h):
        if h == 0:
            x_copy(k).wait_recv()
        y_copy(k, h).wait_recv()
        g_ref[k, :, cols(h)] = g_ref[k, :, cols(h)] + outer(xr_ref[k], yr_ref[k, :, cols(h)])
        start(wing_copy(k, h))

    def s2(k, h):
        b = routes[k][1]
        wing_copy(k, h).wait_recv()
        t_ref[k, :, cols(h)] = g_ref[k, pl.ds(b * band, band), cols(h)] + r1_ref[k, :, cols(h)]
        for j in range(1, lines):
            start(line_copy(k, h, j))

    def s3(k, h):
        total = t_ref[k, pl.ds(z * rows, rows), cols(h)]
        for j in range(1, lines):
            line_copy(k, h, j).wait_recv()
            total = total + r2_ref[k, j - 1, :, cols(h)]
        own_ref[k, :, cols(h)] = total.astype(BF16)

    pl.semaphore_wait(barrier, len(partners))
    for k in range(mine):
        start(x_copy(k))
    for h in range(PARTS):
        for k in range(mine):
            start(y_copy(k, h))
    for i, (src, dst) in enumerate(stored):
        start(remote(src, dst.at[own], pre_send.at[i], pre_recv.at[i], core_mate))
    for k in range(mine):
        g_ref[k] = outer(x_ref[:, wing_of(k, routes[k][0])], y_ref[:, k * size:(k + 1) * size])

    index = scalar_places(assign_ref, blocks, capacity)
    target = scalar_places(owner_ref, blocks, capacity)
    slots = 2 * capacity

    local_index = [jnp.where(core == 0, index[k], index[mine + k]) for k in range(mine)]

    def select():
        for copy in local:
            copy.wait()
        for i, (src, dst) in enumerate(stored):
            remote(src, dst.at[theirs], pre_send.at[i], pre_recv.at[i], core_mate).wait_recv()
        for k in range(mine):
            picks = [hot(local_index[k], s) for s in range(slots)]

            def pick(at, _, k=k, picks=picks):
                part = pl.ds(pl.multiple_of(at * 64, 64), 64)
                chosen = right_ref[0, part, :].astype(F32) * picks[0]
                for s in range(1, slots):
                    chosen = chosen + right_ref[s, part, :].astype(F32) * picks[s]
                rsel_ref[k, part, :] = chosen.astype(BF16)
                return 0

            lax.fori_loop(0, size // 64, pick, 0)
            chosen = left_ref[0].astype(F32) * picks[0]
            for s in range(1, slots):
                chosen = chosen + left_ref[s].astype(F32) * picks[s]
            lband_ref[q, k] = chosen.astype(BF16)
        for k in range(blocks):
            moment = mom_ref[0] * hot(index[k], 0)
            for s in range(1, slots):
                moment = moment + mom_ref[s] * hot(index[k], s)
            msel_ref[k] = moment

    def left_copy(j, place):
        part = lband_ref.at[place]
        return remote(part, part, left_send.at[j - 1], left_recv.at[j - 1], plane_mate(j))

    def half_copy(j, place):
        device = lax.rem(me + j, n_dp)
        src = hb_ref.at[lax.rem(device, PLANE)]
        return remote(src, hall_ref.at[place], half_send.at[j - 1], half_recv.at[j - 1], (device, core))

    def both_copy(j, place):
        src = bo_ref.at[lax.rem(q + j, PLANE)]
        return remote(src, both_ref.at[core, place], both_send.at[j - 1], both_recv.at[j - 1], plane_mate(j))

    def core_copy(j, at):
        part = both_ref.at[at, lax.rem(q + PLANE - j, PLANE)]
        return remote(part, part, fw_send.at[j], fw_recv.at[j], core_mate)

    def p_copy(j):
        device = (lax.rem(me + j, n_dp), core)
        return remote(p_ref, pr_ref.at[j - 1], p_send.at[j - 1], p_recv.at[j - 1], device)

    def lanes(value):
        partial = value[:, 0:128]
        for at in range(128, value.shape[1], 128):
            partial = partial + value[:, at:at + 128]
        return jnp.sum(partial, axis=0, keepdims=True)

    order = [(k, h) for h in range(PARTS) for k in range(mine)]
    stages = (s1, s2, s3)
    for step in range(len(order) + len(stages) - 1):
        for late in range(len(stages)):
            if 0 <= step - late < len(order):
                stages[late](*order[step - late])
        if step == 1:
            select()
        if step == len(order):
            for j in range(1, PLANE):
                left_copy(j, q).start()

    p_ref[...] = jnp.zeros_like(p_ref)
    for k in range(mine):
        half = jnp.dot(own_ref[k], rsel_ref[k], preferred_element_type=F32).astype(BF16)
        for j in range(PLANE):
            hb_ref[j, k] = half[:, j * band:(j + 1) * band]
    for j in range(1, n_dp):
        half_copy(j, me).start()
    hall_ref[me] = hb_ref[q]
    for k in range(mine):
        value = own_ref[k].astype(F32)
        p_ref[mine + k:mine + k + 1, :] = lanes(value * value)
    for j in range(1, PLANE):
        left_copy(j, lax.rem(q + PLANE - j, PLANE)).wait_recv()
    for j in range(1, n_dp):
        half_copy(j, lax.rem(me + n_dp - j, n_dp)).wait_recv()
    for device in range(n_dp):
        line, corner = divmod(device, PLANE)
        for k in range(mine):
            a, b = (corner % 2, corner // 2) if k % 2 == 0 else (corner // 2, corner % 2)
            first = (a * 2 + b) * band + line * rows
            hfull_ref[k, first:first + rows, :] = hall_ref[device, k]
    for k in range(mine):
        square = jnp.zeros((1, 128), F32)
        for j in range(PLANE):
            value = jnp.dot(lband_ref[j, k], hfull_ref[k], preferred_element_type=F32)
            bo_ref[j, k] = value
            square = square + lanes(value * value)
        p_ref[k:k + 1, :] = square
    for j in range(1, n_dp):
        p_copy(j).start()
    for j in range(1, PLANE):
        both_copy(j, q).start()
    both_ref[core, q] = bo_ref[q]
    core_copy(0, core).start()
    for j in range(1, PLANE):
        both_copy(j, lax.rem(q + PLANE - j, PLANE)).wait_recv()
        core_copy(j, core).start()
    total = p_ref[...]
    for j in range(1, n_dp):
        p_copy(j).wait_recv()
        total = total + pr_ref[j - 1]
    sum_ref[core] = total
    sum_mine, sum_theirs = sum_ref.at[core], sum_ref.at[other]
    remote(sum_mine, sum_mine, sum_send.at[0], sum_recv.at[0], core_mate).start()
    for j in range(PLANE):
        core_copy(j, other).wait_recv()
    remote(sum_theirs, sum_theirs, sum_send.at[0], sum_recv.at[0], core_mate).wait_recv()

    factors = []
    for k in range(blocks):
        sums = jnp.sum(sum_ref[k // mine], axis=1, keepdims=True)
        at = k % mine
        factors.append(jnp.sqrt(sums[mine + at:mine + at + 1] / (sums[at:at + 1] + EPS)))
    for j in range(PLANE):
        part = slice(j * band, (j + 1) * band)
        grafted = [both_ref[k // mine, j, k % mine] * factors[k] for k in range(blocks)]
        moved = [(BETA * msel_ref[k, :, part] + grafted[k]).astype(BF16).astype(F32) for k in range(blocks)]
        for s in range(capacity):
            here = core * capacity + s
            value = BETA * mom_ref[here, :, part]
            update = jnp.zeros((rows, band), F32)
            for k in range(blocks):
                value = value + grafted[k] * hot(index[k], here)
                update = update + moved[k] * hot(target[k], here)
            mom_out[s, :, part] = value
            upd_out[s, :, part] = update.astype(BF16)
    for j in range(1, PLANE):
        left_copy(j, q).wait_send()
        both_copy(j, q).wait_send()
    for j in range(1, n_dp):
        half_copy(j, me).wait_send()
        p_copy(j).wait_send()
    for j in range(PLANE):
        core_copy(j, core).wait_send()
    remote(sum_mine, sum_mine, sum_send.at[0], sum_recv.at[0], core_mate).wait_send()
    for copy in sends:
        copy.wait_send()


def fused(n_dp, inputs_blk, grads_out, assign, param_owner, left_root, right_root, momentum):
    tokens, mine, size = inputs_blk.shape
    capacity = right_root.shape[0]
    blocks = assign.shape[0]
    rows = size // n_dp
    band, wing, lines = size // PLANE, size // 2, n_dp // PLANE
    slots = 2 * capacity
    vmem = pl.BlockSpec(memory_space=pltpu.VMEM)
    smem = pl.BlockSpec(memory_space=pltpu.SMEM)
    anyw = pl.BlockSpec(memory_space=pl.ANY)
    dma = pltpu.SemaphoreType.DMA
    flops = 2 * mine * tokens * size * size + 2 * blocks * size**3
    return pl.pallas_call(
        functools.partial(kernel, (n_dp, mine, blocks, capacity, size)),
        out_shape=(
            jax.ShapeDtypeStruct((capacity, rows, size), F32),
            jax.ShapeDtypeStruct((capacity, rows, size), BF16),
        ),
        in_specs=[vmem, vmem, smem, smem, anyw, anyw, anyw],
        out_specs=(vmem, vmem),
        scratch_shapes=[
            pltpu.VMEM((mine, tokens, wing), BF16),
            pltpu.VMEM((mine, tokens, size), BF16),
            pltpu.VMEM((mine, wing, size), F32),
            pltpu.VMEM((mine, band, size), F32),
            pltpu.VMEM((mine, band, size), F32),
            pltpu.VMEM((mine, lines - 1, rows, size), F32),
            pltpu.VMEM((mine, rows, size), BF16),
            pltpu.VMEM((slots, size, size), BF16),
            pltpu.VMEM((slots, rows, size), BF16),
            pltpu.VMEM((slots, rows, size), F32),
            pltpu.VMEM((mine, size, size), BF16),
            pltpu.VMEM((PLANE, mine, rows, size), BF16),
            pltpu.VMEM((blocks, rows, size), F32),
            pltpu.VMEM((PLANE, mine, rows, band), BF16),
            pltpu.VMEM((n_dp, mine, rows, band), BF16),
            pltpu.VMEM((mine, size, band), BF16),
            pltpu.VMEM((PLANE, mine, rows, band), F32),
            pltpu.VMEM((2, PLANE, mine, rows, band), F32),
            pltpu.VMEM((8, 128), F32),
            pltpu.VMEM((n_dp - 1, 8, 128), F32),
            pltpu.VMEM((2, 8, 128), F32),
            dma((3,)), dma((3,)), dma((3,)),
            dma((mine,)), dma((mine,)),
            dma((mine, PARTS)), dma((mine, PARTS)),
            dma((mine, PARTS)), dma((mine, PARTS)),
            dma((mine, PARTS, lines - 1)), dma((mine, PARTS, lines - 1)),
            dma((PLANE - 1,)), dma((PLANE - 1,)),
            dma((n_dp - 1,)), dma((n_dp - 1,)),
            dma((PLANE - 1,)), dma((PLANE - 1,)),
            dma((PLANE,)), dma((PLANE,)),
            dma((n_dp - 1,)), dma((n_dp - 1,)),
            dma((1,)), dma((1,)),
        ],
        compiler_params=pltpu.CompilerParams(
            collective_id=0, has_side_effects=True, vmem_limit_bytes=40 * 1024 * 1024
        ),
        cost_estimate=pl.CostEstimate(flops=flops, bytes_accessed=4 * 1024 * 1024, transcendentals=0),
    )(
        inputs_blk.reshape(tokens, mine * size),
        grads_out.reshape(tokens, mine * size),
        assign, param_owner, left_root, right_root, momentum,
    )


def general(inputs_blk, grads_out, assign, param_owner, left_root, right_root, momentum):
    capacity = right_root.shape[0]
    blocks = assign.shape[0]
    my_index = lax.axis_index("mp")
    reduced = lax.psum_scatter(
        jnp.einsum("tkr,tkc->rkc", inputs_blk, grads_out, preferred_element_type=F32),
        "dp",
        scatter_dimension=0,
        tiled=True,
    )
    rounded = reduced.astype(BF16)
    gathered = lax.all_gather(rounded, "mp", axis=1, tiled=True)
    slot = slots_of(assign)
    slot_ids = lax.broadcasted_iota(jnp.int32, (capacity, blocks), 0)
    chooser = ((assign[None, :] == my_index) & (slot[None, :] == slot_ids)).astype(BF16)
    owned = jnp.einsum("ck,rkb->crb", chooser, gathered, preferred_element_type=F32).astype(BF16)
    half = jnp.einsum("crb,cbe->cre", owned, right_root, preferred_element_type=F32).astype(BF16)
    both = jnp.einsum(
        "cri,cie->cre",
        left_root,
        lax.all_gather(half, "dp", axis=1, tiled=True),
        preferred_element_type=F32,
    )
    grad_square = jnp.sum(jnp.square(owned.astype(F32)), axis=(1, 2))
    prec_square = jnp.sum(both * both, axis=(1, 2))
    grad_square, prec_square = lax.psum((grad_square, prec_square), "dp")
    factor = jnp.sqrt(grad_square / (prec_square + EPS))
    moved = BETA * momentum + both * factor[:, None, None]
    sending = moved.astype(BF16)
    pooled = lax.all_gather(sending, "mp", axis=0, tiled=True)
    place = slots_of(param_owner)
    source = assign * capacity + slot
    target_hot = ((param_owner[None, :] == my_index) & (place[None, :] == slot_ids)).astype(F32)
    pool_ids = lax.broadcasted_iota(jnp.int32, (blocks, pooled.shape[0]), 1)
    source_hot = (source[:, None] == pool_ids).astype(F32)
    mover = jnp.dot(target_hot, source_hot, preferred_element_type=F32).astype(BF16)
    update = jnp.einsum("qs,srb->qrb", mover, pooled, preferred_element_type=F32).astype(BF16)
    return (moved, update)


def solution(mesh):
    n_dp, n_mp = mesh.shape["dp"], mesh.shape["mp"]

    def on_device(inputs_blk, *rest):
        rows = inputs_blk.shape[2] // n_dp
        if n_mp == 2 and n_dp % PLANE == 0 and rows % 16 == 0 and inputs_blk.shape[1] == 2:
            return fused(n_dp, inputs_blk, *rest)
        return general(inputs_blk, *rest)

    placed = (
        P("dp", "mp", None),
        P("dp", "mp", None),
        P(),
        P(),
        P("mp", "dp", None),
        P("mp", None, None),
        P("mp", "dp", None),
    )
    return jax.shard_map(
        on_device,
        mesh=mesh,
        in_specs=placed,
        out_specs=(P("mp", "dp", None), P("mp", "dp", None)),
        check_vma=False,
    )
```

time: 230 us -> 53 us (0.23)
  blocking collectives: 146 us -> 0 us
  waiting for transfers between devices: 55.1 us -> 0 us
  Pallas kernels: 0 us -> 48.4 us
  between operations: 14.8 us -> 0.73 us
  matrix products: 6.81 us -> 0 us
    unnamed x1 -> x0, blocking collectives: 94 us -> none
    all_gather x1 -> x0, waiting for transfers between devices: 55.1 us -> none  [on_device(): lax.all_gather(half, 'dp', axis=1, tiled=True)]
    pallas_call x0 -> x1, Pallas kernels: none -> 48.4 us  [fused(): pl.pallas_call(functools.partial(kernel, (n_dp, mine, blocks, capacity, s...]
    psum x1 -> x0, blocking collectives: 31.8 us -> none  [on_device(): grad_square, prec_square = lax.psum((grad_square, prec_square), 'dp')]
    all_gather x2 -> x0, blocking collectives: 20.5 us -> none  [the longest x1 11.5 us: on_device(): pooled = lax.all_gather(sending, 'mp', axis=0, tiled=True)]
    dot_general x5 -> x0, matrix products: 6.81 us -> none  [the longest x1 3.15 us: on_device(): jnp.einsum('tkr,tkc->rkc', window, grads_out, preferred_element_type=jnp....]
    transpose x1 -> x0, local copies, waits for them, and re-layouts: 4.13 us -> none  [on_device(): jnp.einsum('tkr,tkc->rkc', window, grads_out, preferred_element_type=jnp....]
    unnamed x14, local copies, waits for them, and re-layouts: 1.28 us -> 3.69 us
  transfers between devices with their start and end apart: 1 -> 0, of which waited for: 1 -> 0; matrix products, arithmetic and copies ran while one was open for 0% -> 0% of each run, Pallas kernels for 0% -> 0%
where the time goes in v2:
time: 53 us; the launch traced here: 52.8 us
  Pallas kernels  48.4 us (91%)
  local copies, waits for them, and re-layouts  3.69 us (7%)
  between operations  0.73 us (1%)
    pallas_call x1, Pallas kernels, fused(): pl.pallas_call(functools.partial(kernel, (n_dp, mine, blocks, capacity, s...  48.4 us
    unnamed x14, local copies, waits for them, and re-layouts  3.69 us

profile of v2, /device:TPU:1, one launch (start us, length us, event | category | flops | bytes accessed | tf_op | source)
XLA Modules:
  0.0 52.8 jit_solution(1436755510909205574)
XLA Ops:
  0.6 0.0 copy-start.1
  0.6 0.0 copy-start
  0.7 0.0 copy-start.2
  0.7 0.0 copy-start.4
  0.7 0.0 copy-start.3
  0.7 1.2 %copy.9 = bf16[32,8,2,512]{3,1,2,0:T(8,128)(2,1)S(1)} copy(bf16[32,8,2,512]{3,2,1,0:T(2,128)(2,1)} %bitcast.6) | data formatting | bytes 1048576
  1.9 1.1 %copy.10 = bf16[32,8,2,512]{3,1,2,0:T(8,128)(2,1)S(1)} copy(bf16[32,8,2,512]{3,2,1,0:T(2,128)(2,1)} %bitcast.7) | data formatting | bytes 1048576
  3.0 0.0 copy-done.1
  3.1 0.0 copy-done
  3.1 0.0 copy-done.2
  3.1 0.0 copy-done.4
  3.1 0.0 copy-done.3
  3.1 48.4 %shard_map.86 = (f32[3,32,512]{2,1,0:T(8,128)S(1)}, bf16[3,32,512]{2,1,0:T(8,128)(2,1)S(1)}) custom-call(bf16[256,1024]{1,0:T(8,128)(2,1)S(1)} %bitcast.4, bf16[256,1024]{1,0:T(8,128)(2,1)S(1)} %bitcast.5, s32[4]{0:T(128)S(1)} %copy-done.3, s32[4]{0:T(128)S(1)} %copy-done.4, bf16[3,32,512]{2,1,0:T(8,128)(2,1)S(1)} %copy-done.2, ...), custom_call_target="tpu_custom_call" | custom-call | flops 1342177280 | bytes 4194304 | tf_op jit(solution)/shard_map/pallas_call | solution.py:323
  51.5 0.7 %copy.13 = f32[3,32,512]{2,1,0:T(8,128)} copy(f32[3,32,512]{2,1,0:T(8,128)S(1)} %get-tuple-element.4) | data formatting | bytes 393216
  52.2 0.6 %copy.14 = bf16[3,32,512]{2,1,0:T(8,128)(2,1)} copy(bf16[3,32,512]{2,1,0:T(8,128)(2,1)S(1)} %get-tuple-element.5) | data formatting | bytes 196608
Async XLA Ops:
  0.6 2.4 %copy-start.1 = (f32[3,32,512]{2,1,0:T(8,128)S(1)}, f32[3,32,512]{2,1,0:T(8,128)}, u32[]{:S(2)}) copy-start(f32[3,32,512]{2,1,0:T(8,128)} %mom_hbm.1) | copy-start | bytes 589828
  0.6 2.4 %copy-start = (bf16[3,512,512]{2,1,0:T(8,128)(2,1)S(1)}, bf16[3,512,512]{2,1,0:T(8,128)(2,1)}, u32[]{:S(2)}) copy-start(bf16[3,512,512]{2,1,0:T(8,128)(2,1)} %right_hbm.1) | copy-start | bytes 4718596
  0.7 2.4 %copy-start.2 = (bf16[3,32,512]{2,1,0:T(8,128)(2,1)S(1)}, bf16[3,32,512]{2,1,0:T(8,128)(2,1)}, u32[]{:S(2)}) copy-start(bf16[3,32,512]{2,1,0:T(8,128)(2,1)} %left_hbm.1) | copy-start | bytes 294916
  0.7 2.4 %copy-start.4 = (s32[4]{0:T(128)S(1)}, s32[4]{0:T(128)}, u32[]{:S(2)}) copy-start(s32[4]{0:T(128)} %owner_ref.1) | copy-start | bytes 52
  0.7 2.4 %copy-start.3 = (s32[4]{0:T(128)S(1)}, s32[4]{0:T(128)}, u32[]{:S(2)}) copy-start(s32[4]{0:T(128)} %assign_ref.1) | copy-start | bytes 52

commit v3 on v2

--- a/solution.py
+++ b/solution.py
@@ -131,6 +131,8 @@
         y_copy(k, h).wait_recv()
         g_ref[k, :, cols(h)] = g_ref[k, :, cols(h)] + outer(xr_ref[k], yr_ref[k, :, cols(h)])
         start(wing_copy(k, h))
+        if h + 1 < PARTS:
+            start(y_copy(k, h + 1))
 
     def s2(k, h):
         b = routes[k][1]
@@ -149,9 +151,8 @@
     pl.semaphore_wait(barrier, len(partners))
     for k in range(mine):
         start(x_copy(k))
-    for h in range(PARTS):
-        for k in range(mine):
-            start(y_copy(k, h))
+    for k in range(mine):
+        start(y_copy(k, 0))
     for i, (src, dst) in enumerate(stored):
         start(remote(src, dst.at[own], pre_send.at[i], pre_recv.at[i], core_mate))
     for k in range(mine):
@@ -217,17 +218,20 @@
             partial = partial + value[:, at:at + 128]
         return jnp.sum(partial, axis=0, keepdims=True)
 
-    order = [(k, h) for h in range(PARTS) for k in range(mine)]
-    stages = (s1, s2, s3)
-    for step in range(len(order) + len(stages) - 1):
-        for late in range(len(stages)):
-            if 0 <= step - late < len(order):
-                stages[late](*order[step - late])
+    for step in range(PARTS + 0):
+        if step < PARTS:
+            for k in range(mine):
+                s1(k, step)
+        if step >= 0:
+            for k in range(mine):
+                s2(k, step - 0)
         if step == 1:
             select()
-        if step == len(order):
-            for j in range(1, PLANE):
-                left_copy(j, q).start()
+    for j in range(1, PLANE):
+        left_copy(j, q).start()
+    for h in range(PARTS):
+        for k in range(mine):
+            s3(k, h)
 
     p_ref[...] = jnp.zeros_like(p_ref)
     for k in range(mine):

time: 53 us -> 49.2 us (0.928)
  Pallas kernels: 48.4 us -> 44.6 us
    pallas_call x1, Pallas kernels: 48.4 us -> 44.6 us  [fused(): pl.pallas_call(functools.partial(kernel, (n_dp, mine, blocks, capacity, s...]
where the time goes in v3:
time: 49.2 us; the launch traced here: 49 us
  Pallas kernels  44.6 us (91%)
  local copies, waits for them, and re-layouts  3.69 us (8%)
  between operations  0.73 us (1%)
    pallas_call x1, Pallas kernels, fused(): pl.pallas_call(functools.partial(kernel, (n_dp, mine, blocks, capacity, s...  44.6 us
    unnamed x14, local copies, waits for them, and re-layouts  3.69 us

profile of v3, /device:TPU:1, one launch (start us, length us, event | category | flops | bytes accessed | tf_op | source)
XLA Modules:
  0.0 49.0 jit_solution(6892723364299280297)
XLA Ops:
  0.6 0.0 copy-start.1
  0.6 0.0 copy-start
  0.7 0.0 copy-start.2
  0.7 0.0 copy-start.4
  0.7 0.0 copy-start.3
  0.7 1.2 %copy.9 = bf16[32,8,2,512]{3,1,2,0:T(8,128)(2,1)S(1)} copy(bf16[32,8,2,512]{3,2,1,0:T(2,128)(2,1)} %bitcast.6) | data formatting | bytes 1048576
  1.9 1.1 %copy.10 = bf16[32,8,2,512]{3,1,2,0:T(8,128)(2,1)S(1)} copy(bf16[32,8,2,512]{3,2,1,0:T(2,128)(2,1)} %bitcast.7) | data formatting | bytes 1048576
  3.0 0.0 copy-done.1
  3.1 0.0 copy-done
  3.1 0.0 copy-done.2
  3.1 0.0 copy-done.4
  3.1 0.0 copy-done.3
  3.1 44.6 %shard_map.86 = (f32[3,32,512]{2,1,0:T(8,128)S(1)}, bf16[3,32,512]{2,1,0:T(8,128)(2,1)S(1)}) custom-call(bf16[256,1024]{1,0:T(8,128)(2,1)S(1)} %bitcast.4, bf16[256,1024]{1,0:T(8,128)(2,1)S(1)} %bitcast.5, s32[4]{0:T(128)S(1)} %copy-done.3, s32[4]{0:T(128)S(1)} %copy-done.4, bf16[3,32,512]{2,1,0:T(8,128)(2,1)S(1)} %copy-done.2, ...), custom_call_target="tpu_custom_call" | custom-call | flops 1342177280 | bytes 4194304 | tf_op jit(solution)/shard_map/pallas_call | solution.py:327
  47.7 0.7 %copy.13 = f32[3,32,512]{2,1,0:T(8,128)} copy(f32[3,32,512]{2,1,0:T(8,128)S(1)} %get-tuple-element.4) | data formatting | bytes 393216
  48.4 0.6 %copy.14 = bf16[3,32,512]{2,1,0:T(8,128)(2,1)} copy(bf16[3,32,512]{2,1,0:T(8,128)(2,1)S(1)} %get-tuple-element.5) | data formatting | bytes 196608
Async XLA Ops:
  0.6 2.4 %copy-start.1 = (f32[3,32,512]{2,1,0:T(8,128)S(1)}, f32[3,32,512]{2,1,0:T(8,128)}, u32[]{:S(2)}) copy-start(f32[3,32,512]{2,1,0:T(8,128)} %mom_hbm.1) | copy-start | bytes 589828
  0.6 2.4 %copy-start = (bf16[3,512,512]{2,1,0:T(8,128)(2,1)S(1)}, bf16[3,512,512]{2,1,0:T(8,128)(2,1)}, u32[]{:S(2)}) copy-start(bf16[3,512,512]{2,1,0:T(8,128)(2,1)} %right_hbm.1) | copy-start | bytes 4718596
  0.7 2.4 %copy-start.2 = (bf16[3,32,512]{2,1,0:T(8,128)(2,1)S(1)}, bf16[3,32,512]{2,1,0:T(8,128)(2,1)}, u32[]{:S(2)}) copy-start(bf16[3,32,512]{2,1,0:T(8,128)(2,1)} %left_hbm.1) | copy-start | bytes 294916
  0.7 2.4 %copy-start.4 = (s32[4]{0:T(128)S(1)}, s32[4]{0:T(128)}, u32[]{:S(2)}) copy-start(s32[4]{0:T(128)} %owner_ref.1) | copy-start | bytes 52
  0.7 2.4 %copy-start.3 = (s32[4]{0:T(128)S(1)}, s32[4]{0:T(128)}, u32[]{:S(2)}) copy-start(s32[4]{0:T(128)} %assign_ref.1) | copy-start | bytes 52

commit v4 on v3

--- a/solution.py
+++ b/solution.py
@@ -46,13 +46,15 @@
     local_sem, pre_send, pre_recv, x_send, x_recv, y_send, y_recv, s1_send, s1_recv, s2_send, s2_recv,
     left_send, left_recv, half_send, half_recv, both_send, both_recv, fw_send, fw_recv,
     p_send, p_recv, sum_send, sum_recv,
+    gz_ref, rz_ref, tz_ref, uz_ref, gz_send, gz_recv, tz_send, tz_recv,
 ):
     n_dp, mine, blocks, capacity, size = dims
     lines = n_dp // PLANE
     rows = size // n_dp
     band = size // PLANE
     wing = size // 2
-    width = size // PARTS
+    tail = size // 4
+    starts, widths = (0, size // 4), (size // 4, size // 2)
     me = lax.axis_index("dp")
     core = lax.axis_index("mp")
     q = lax.rem(me, PLANE)
@@ -102,7 +104,7 @@
         return lax.dot_general(x, y, (((0,), (0,)), ((), ())), preferred_element_type=F32)
 
     def cols(h):
-        return slice(h * width, (h + 1) * width)
+        return slice(starts[h], starts[h] + widths[h])
 
     def wing_of(k, a):
         return pl.ds(pl.multiple_of(k * size + a * wing, wing), wing)
@@ -112,17 +114,17 @@
         return remote(x_ref.at[:, wing_of(k, 1 - a)], xr_ref.at[k], x_send.at[k], x_recv.at[k], mate)
 
     def y_copy(k, h):
-        src = y_ref.at[:, pl.ds(k * size + h * width, width)]
-        return remote(src, yr_ref.at[k, :, pl.ds(h * width, width)], y_send.at[k, h], y_recv.at[k, h], routes[k][2])
+        src = y_ref.at[:, pl.ds(k * size + starts[h], widths[h])]
+        return remote(src, yr_ref.at[k, :, pl.ds(starts[h], widths[h])], y_send.at[k, h], y_recv.at[k, h], routes[k][2])
 
     def wing_copy(k, h):
         _, b, _, mate = routes[k]
-        src = g_ref.at[k, pl.ds((1 - b) * band, band), pl.ds(h * width, width)]
-        return remote(src, r1_ref.at[k, :, pl.ds(h * width, width)], s1_send.at[k, h], s1_recv.at[k, h], mate)
+        src = g_ref.at[k, pl.ds((1 - b) * band, band), pl.ds(starts[h], widths[h])]
+        return remote(src, r1_ref.at[k, :, pl.ds(starts[h], widths[h])], s1_send.at[k, h], s1_recv.at[k, h], mate)
 
     def line_copy(k, h, j):
-        src = t_ref.at[k, pl.ds(lax.rem(z + j, lines) * rows, rows), pl.ds(h * width, width)]
-        dst = r2_ref.at[k, j - 1, :, pl.ds(h * width, width)]
+        src = t_ref.at[k, pl.ds(lax.rem(z + j, lines) * rows, rows), pl.ds(starts[h], widths[h])]
+        dst = r2_ref.at[k, j - 1, :, pl.ds(starts[h], widths[h])]
         return remote(src, dst, s2_send.at[k, h, j - 1], s2_recv.at[k, h, j - 1], at_line(j))
 
     def s1(k, h):
@@ -148,15 +150,34 @@
             total = total + r2_ref[k, j - 1, :, cols(h)]
         own_ref[k, :, cols(h)] = total.astype(BF16)
 
+    def corner_band(k, corner):
+        return corner % 2 * 2 + corner // 2 if k % 2 == 0 else corner
+
+    def gz_copy(j):
+        place = lax.rem(z + j, lines)
+        return remote(gz_ref.at[place], rz_ref.at[j - 1], gz_send.at[j - 1], gz_recv.at[j - 1], at_line(j))
+
+    def tz_copy(j):
+        place = lax.rem(q + j, PLANE)
+        return remote(tz_ref.at[place], uz_ref.at[j - 1], tz_send.at[j - 1], tz_recv.at[j - 1], plane_mate(j))
+
+    for k in range(mine):
+        value = outer(x_ref[:, k * size:(k + 1) * size], y_ref[:, (k + 1) * size - tail:(k + 1) * size])
+        for at in range(PLANE):
+            for line in range(lines):
+                first = at * band + line * rows
+                gz_ref[line, k, at] = value[first:first + rows]
     pl.semaphore_wait(barrier, len(partners))
     for k in range(mine):
         start(x_copy(k))
     for k in range(mine):
         start(y_copy(k, 0))
+    for j in range(1, lines):
+        start(gz_copy(j))
     for i, (src, dst) in enumerate(stored):
         start(remote(src, dst.at[own], pre_send.at[i], pre_recv.at[i], core_mate))
     for k in range(mine):
-        g_ref[k] = outer(x_ref[:, wing_of(k, routes[k][0])], y_ref[:, k * size:(k + 1) * size])
+        g_ref[k] = outer(x_ref[:, wing_of(k, routes[k][0])], y_ref[:, k * size:(k + 1) * size - tail])
 
     index = scalar_places(assign_ref, blocks, capacity)
     target = scalar_places(owner_ref, blocks, capacity)
@@ -227,11 +248,29 @@
                 s2(k, step - 0)
         if step == 1:
             select()
+    for j in range(1, lines):
+        gz_copy(j).wait_recv()
+    for corner in range(PLANE):
+        for k in range(mine):
+            at = corner_band(k, corner)
+            total = gz_ref[z, k, at]
+            for j in range(1, lines):
+                total = total + rz_ref[j - 1, k, at]
+            tz_ref[corner, k] = total
+    for j in range(1, PLANE):
+        start(tz_copy(j))
     for j in range(1, PLANE):
         left_copy(j, q).start()
     for h in range(PARTS):
         for k in range(mine):
             s3(k, h)
+    for j in range(1, PLANE):
+        tz_copy(j).wait_recv()
+    for k in range(mine):
+        total = tz_ref[q, k]
+        for j in range(1, PLANE):
+            total = total + uz_ref[j - 1, k]
+        own_ref[k, :, size - tail:size] = total.astype(BF16)
 
     p_ref[...] = jnp.zeros_like(p_ref)
     for k in range(mine):
@@ -335,7 +374,7 @@
         scratch_shapes=[
             pltpu.VMEM((mine, tokens, wing), BF16),
             pltpu.VMEM((mine, tokens, size), BF16),
-            pltpu.VMEM((mine, wing, size), F32),
+            pltpu.VMEM((mine, wing, size - size // 4), F32),
             pltpu.VMEM((mine, band, size), F32),
             pltpu.VMEM((mine, band, size), F32),
             pltpu.VMEM((mine, lines - 1, rows, size), F32),
@@ -365,6 +404,12 @@
             dma((PLANE,)), dma((PLANE,)),
             dma((n_dp - 1,)), dma((n_dp - 1,)),
             dma((1,)), dma((1,)),
+            pltpu.VMEM((lines, mine, PLANE, rows, size // 4), F32),
+            pltpu.VMEM((lines - 1, mine, PLANE, rows, size // 4), F32),
+            pltpu.VMEM((PLANE, mine, rows, size // 4), F32),
+            pltpu.VMEM((PLANE - 1, mine, rows, size // 4), F32),
+            dma((lines - 1,)), dma((lines - 1,)),
+            dma((PLANE - 1,)), dma((PLANE - 1,)),
         ],
         compiler_params=pltpu.CompilerParams(
             collective_id=0, has_side_effects=True, vmem_limit_bytes=40 * 1024 * 1024

time: 49.2 us -> 46.9 us (0.953)
  Pallas kernels: 44.6 us -> 42.3 us
    pallas_call x1, Pallas kernels: 44.6 us -> 42.3 us  [fused(): pl.pallas_call(functools.partial(kernel, (n_dp, mine, blocks, capacity, s...]
where the time goes in v4:
time: 46.9 us; the launch traced here: 46.7 us
  Pallas kernels  42.3 us (90%)
  local copies, waits for them, and re-layouts  3.69 us (8%)
  between operations  0.73 us (2%)
    pallas_call x1, Pallas kernels, fused(): pl.pallas_call(functools.partial(kernel, (n_dp, mine, blocks, capacity, s...  42.3 us
    unnamed x14, local copies, waits for them, and re-layouts  3.69 us

profile of v4, /device:TPU:1, one launch (start us, length us, event | category | flops | bytes accessed | tf_op | source)
XLA Modules:
  0.0 46.7 jit_solution(17859143851793198025)
XLA Ops:
  0.6 0.0 copy-start.1
  0.6 0.0 copy-start
  0.7 0.0 copy-start.2
  0.7 0.0 copy-start.4
  0.7 0.0 copy-start.3
  0.7 1.2 %copy.9 = bf16[32,8,2,512]{3,1,2,0:T(8,128)(2,1)S(1)} copy(bf16[32,8,2,512]{3,2,1,0:T(2,128)(2,1)} %bitcast.6) | data formatting | bytes 1048576
  1.9 1.1 %copy.10 = bf16[32,8,2,512]{3,1,2,0:T(8,128)(2,1)S(1)} copy(bf16[32,8,2,512]{3,2,1,0:T(2,128)(2,1)} %bitcast.7) | data formatting | bytes 1048576
  3.0 0.0 copy-done.1
  3.1 0.0 copy-done
  3.1 0.0 copy-done.2
  3.1 0.0 copy-done.4
  3.1 0.0 copy-done.3
  3.1 42.3 %shard_map.86 = (f32[3,32,512]{2,1,0:T(8,128)S(1)}, bf16[3,32,512]{2,1,0:T(8,128)(2,1)S(1)}) custom-call(bf16[256,1024]{1,0:T(8,128)(2,1)S(1)} %bitcast.4, bf16[256,1024]{1,0:T(8,128)(2,1)S(1)} %bitcast.5, s32[4]{0:T(128)S(1)} %copy-done.3, s32[4]{0:T(128)S(1)} %copy-done.4, bf16[3,32,512]{2,1,0:T(8,128)(2,1)S(1)} %copy-done.2, ...), custom_call_target="tpu_custom_call" | custom-call | flops 1342177280 | bytes 4194304 | tf_op jit(solution)/shard_map/pallas_call | solution.py:366
  45.4 0.7 %copy.13 = f32[3,32,512]{2,1,0:T(8,128)} copy(f32[3,32,512]{2,1,0:T(8,128)S(1)} %get-tuple-element.4) | data formatting | bytes 393216
  46.1 0.6 %copy.14 = bf16[3,32,512]{2,1,0:T(8,128)(2,1)} copy(bf16[3,32,512]{2,1,0:T(8,128)(2,1)S(1)} %get-tuple-element.5) | data formatting | bytes 196608
Async XLA Ops:
  0.6 2.4 %copy-start.1 = (f32[3,32,512]{2,1,0:T(8,128)S(1)}, f32[3,32,512]{2,1,0:T(8,128)}, u32[]{:S(2)}) copy-start(f32[3,32,512]{2,1,0:T(8,128)} %mom_hbm.1) | copy-start | bytes 589828
  0.6 2.4 %copy-start = (bf16[3,512,512]{2,1,0:T(8,128)(2,1)S(1)}, bf16[3,512,512]{2,1,0:T(8,128)(2,1)}, u32[]{:S(2)}) copy-start(bf16[3,512,512]{2,1,0:T(8,128)(2,1)} %right_hbm.1) | copy-start | bytes 4718596
  0.7 2.4 %copy-start.2 = (bf16[3,32,512]{2,1,0:T(8,128)(2,1)S(1)}, bf16[3,32,512]{2,1,0:T(8,128)(2,1)}, u32[]{:S(2)}) copy-start(bf16[3,32,512]{2,1,0:T(8,128)(2,1)} %left_hbm.1) | copy-start | bytes 294916
  0.7 2.4 %copy-start.4 = (s32[4]{0:T(128)S(1)}, s32[4]{0:T(128)}, u32[]{:S(2)}) copy-start(s32[4]{0:T(128)} %owner_ref.1) | copy-start | bytes 52
  0.7 2.4 %copy-start.3 = (s32[4]{0:T(128)S(1)}, s32[4]{0:T(128)}, u32[]{:S(2)}) copy-start(s32[4]{0:T(128)} %assign_ref.1) | copy-start | bytes 52

commit v5 on v4

--- a/solution.py
+++ b/solution.py
@@ -168,12 +168,12 @@
                 first = at * band + line * rows
                 gz_ref[line, k, at] = value[first:first + rows]
     pl.semaphore_wait(barrier, len(partners))
-    for k in range(mine):
-        start(x_copy(k))
-    for k in range(mine):
-        start(y_copy(k, 0))
     for j in range(1, lines):
         start(gz_copy(j))
+    for k in range(mine):
+        start(x_copy(k))
+    for k in range(mine):
+        start(y_copy(k, 0))
     for i, (src, dst) in enumerate(stored):
         start(remote(src, dst.at[own], pre_send.at[i], pre_recv.at[i], core_mate))
     for k in range(mine):
@@ -306,9 +306,6 @@
         both_copy(j, q).start()
     both_ref[core, q] = bo_ref[q]
     core_copy(0, core).start()
-    for j in range(1, PLANE):
-        both_copy(j, lax.rem(q + PLANE - j, PLANE)).wait_recv()
-        core_copy(j, core).start()
     total = p_ref[...]
     for j in range(1, n_dp):
         p_copy(j).wait_recv()
@@ -316,6 +313,9 @@
     sum_ref[core] = total
     sum_mine, sum_theirs = sum_ref.at[core], sum_ref.at[other]
     remote(sum_mine, sum_mine, sum_send.at[0], sum_recv.at[0], core_mate).start()
+    for j in range(1, PLANE):
+        both_copy(j, lax.rem(q + PLANE - j, PLANE)).wait_recv()
+        core_copy(j, core).start()
     for j in range(PLANE):
         core_copy(j, other).wait_recv()
     remote(sum_theirs, sum_theirs, sum_send.at[0], sum_recv.at[0], core_mate).wait_recv()

time: 46.9 us -> 47 us (level)
  no operation moved by 1% of the time
where the time goes in v5:
time: 47 us; the launch traced here: 46.8 us
  Pallas kernels  42.4 us (90%)
  local copies, waits for them, and re-layouts  3.69 us (8%)
  between operations  0.73 us (2%)
    pallas_call x1, Pallas kernels, fused(): pl.pallas_call(functools.partial(kernel, (n_dp, mine, blocks, capacity, s...  42.4 us
    unnamed x14, local copies, waits for them, and re-layouts  3.69 us

profile of v5, /device:TPU:1, one launch (start us, length us, event | category | flops | bytes accessed | tf_op | source)
XLA Modules:
  0.0 46.8 jit_solution(7274675157926826197)
XLA Ops:
  0.6 0.0 copy-start.1
  0.6 0.0 copy-start
  0.7 0.0 copy-start.2
  0.7 0.0 copy-start.4
  0.7 0.0 copy-start.3
  0.7 1.2 %copy.9 = bf16[32,8,2,512]{3,1,2,0:T(8,128)(2,1)S(1)} copy(bf16[32,8,2,512]{3,2,1,0:T(2,128)(2,1)} %bitcast.6) | data formatting | bytes 1048576
  1.9 1.1 %copy.10 = bf16[32,8,2,512]{3,1,2,0:T(8,128)(2,1)S(1)} copy(bf16[32,8,2,512]{3,2,1,0:T(2,128)(2,1)} %bitcast.7) | data formatting | bytes 1048576
  3.0 0.0 copy-done.1
  3.1 0.0 copy-done
  3.1 0.0 copy-done.2
  3.1 0.0 copy-done.4
  3.1 0.0 copy-done.3
  3.1 42.4 %shard_map.86 = (f32[3,32,512]{2,1,0:T(8,128)S(1)}, bf16[3,32,512]{2,1,0:T(8,128)(2,1)S(1)}) custom-call(bf16[256,1024]{1,0:T(8,128)(2,1)S(1)} %bitcast.4, bf16[256,1024]{1,0:T(8,128)(2,1)S(1)} %bitcast.5, s32[4]{0:T(128)S(1)} %copy-done.3, s32[4]{0:T(128)S(1)} %copy-done.4, bf16[3,32,512]{2,1,0:T(8,128)(2,1)S(1)} %copy-done.2, ...), custom_call_target="tpu_custom_call" | custom-call | flops 1342177280 | bytes 4194304 | tf_op jit(solution)/shard_map/pallas_call | solution.py:366
  45.5 0.7 %copy.13 = f32[3,32,512]{2,1,0:T(8,128)} copy(f32[3,32,512]{2,1,0:T(8,128)S(1)} %get-tuple-element.4) | data formatting | bytes 393216
  46.2 0.6 %copy.14 = bf16[3,32,512]{2,1,0:T(8,128)(2,1)} copy(bf16[3,32,512]{2,1,0:T(8,128)(2,1)S(1)} %get-tuple-element.5) | data formatting | bytes 196608
Async XLA Ops:
  0.6 2.4 %copy-start.1 = (f32[3,32,512]{2,1,0:T(8,128)S(1)}, f32[3,32,512]{2,1,0:T(8,128)}, u32[]{:S(2)}) copy-start(f32[3,32,512]{2,1,0:T(8,128)} %mom_hbm.1) | copy-start | bytes 589828
  0.6 2.4 %copy-start = (bf16[3,512,512]{2,1,0:T(8,128)(2,1)S(1)}, bf16[3,512,512]{2,1,0:T(8,128)(2,1)}, u32[]{:S(2)}) copy-start(bf16[3,512,512]{2,1,0:T(8,128)(2,1)} %right_hbm.1) | copy-start | bytes 4718596
  0.7 2.4 %copy-start.2 = (bf16[3,32,512]{2,1,0:T(8,128)(2,1)S(1)}, bf16[3,32,512]{2,1,0:T(8,128)(2,1)}, u32[]{:S(2)}) copy-start(bf16[3,32,512]{2,1,0:T(8,128)(2,1)} %left_hbm.1) | copy-start | bytes 294916
  0.7 2.4 %copy-start.4 = (s32[4]{0:T(128)S(1)}, s32[4]{0:T(128)}, u32[]{:S(2)}) copy-start(s32[4]{0:T(128)} %owner_ref.1) | copy-start | bytes 52
  0.7 2.4 %copy-start.3 = (s32[4]{0:T(128)S(1)}, s32[4]{0:T(128)}, u32[]{:S(2)}) copy-start(s32[4]{0:T(128)} %assign_ref.1) | copy-start | bytes 52
